TPU v7x, 32 devices: a whole 2x2x4 slice. The times are simulated.
32 devices in a mesh: cuts: 4 (over y, core), mode: 8 (over z, x).
Axes of the slice: x: 2, y: 2, z: 4, core: 2. Of those that a mesh axis runs over, the one named last changes fastest.
Arguments:
- stem: bfloat16 [4, 2, 1024, 1024], P('cuts', None, None, 'mode'), may hold values from -6 to 6
- branches: bfloat16 [3, 2, 1024, 1024], P(None, None, None, 'mode'), may hold values from -0.125 to 0.125
- order: int32 [3], replicated, may hold values from 0 to 2, each once
- swap_order: int32 [3, 1024], replicated, may hold values from 0 to 1023, each once within a row
- row_bits: int32 [2048], replicated, may hold values from 0 to 1023
- column_bits: int32 [2048], replicated, may hold values from 0 to 1023
Outputs:
- stem_out: bfloat16 [4, 2, 1024, 1024], P('cuts', None, None, 'mode')
- amplitudes: float32 [2, 2048], P(None, ('cuts', 'mode'))
All inputs are finite; a program needn't handle non-finite values.
Results may differ from a plain program's by a relative error of at most 0.009.
Values may be sent and summed in bfloat16 or wider, within the bound.
No kernel may reach another device: no remote copies, remote signals or barrier semaphores. Data moves between devices by JAX's collectives and lax.ppermute only.
A program may use at most 128 MiB of HBM per device.

v0:
```python
import jax
import jax.numpy as jnp
from jax import lax
from jax.sharding import PartitionSpec as P


def absorb(matrix, part):
    numbers = (((0,), (0,)), ((), ()))

    def product(left, right):
        return lax.dot_general(left, right, numbers, preferred_element_type=jnp.float32)

    real = product(matrix[0], part[0]) - product(matrix[1], part[1])
    imag = product(matrix[0], part[1]) + product(matrix[1], part[0])
    return jnp.stack([real, imag], axis=0)


def body(stem, branches, order, swap_order, row_bits, column_bits):
    local = stem[0]
    groups = lax.axis_size("mode")
    width = local.shape[1]
    rows = local.shape[2]
    for step in range(swap_order.shape[0]):
        moved = jnp.take(local, swap_order[step], axis=1)
        view = moved.reshape(2, groups, width // groups, rows)
        swapped = lax.all_to_all(view, "mode", split_axis=1, concat_axis=1, tiled=True)
        current = swapped.reshape(2, width, rows)
        pick = order[step]
        shard = lax.dynamic_index_in_dim(branches, pick, 0, keepdims=False)

        def output_rows(piece, start, source=current):
            return absorb(piece, source).astype(jnp.bfloat16)

        local = output_rows(lax.all_gather(shard, "mode", axis=2, tiled=True), jnp.int32(0))
    offset = lax.axis_index("mode") * rows
    column_local = column_bits - offset
    inside = jnp.logical_and(column_local >= 0, column_local < rows)
    flat_index = row_bits * rows + jnp.clip(column_local, 0, rows - 1)
    flat = local.reshape(2, width * rows)
    values = jnp.take(flat, flat_index, axis=1).astype(jnp.float32)
    values = jnp.where(inside[None, :], values, jnp.zeros_like(values))
    total_amps = lax.psum(values, ("cuts", "mode"))
    share = values.shape[1] // lax.axis_size(("cuts", "mode"))
    amplitudes = lax.dynamic_slice_in_dim(
        total_amps, lax.axis_index(("cuts", "mode")) * share, share, 1
    )
    return (local[None], amplitudes)


def solution(mesh):
    return jax.shard_map(
        body,
        mesh=mesh,
        in_specs=(P("cuts", None, None, "mode"), P(None, None, None, "mode"), P(), P(), P(), P()),
        out_specs=(P("cuts", None, None, "mode"), P(None, ("cuts", "mode"))),
        check_vma=False,
    )
```

profile of v0, /device:TPU:0, one launch (start us, length us, event | category | flops | bytes accessed | tf_op | source)
XLA Modules:
  0.0 385.6 jit_solution(18380586571456264554)
XLA Ops:
  7.2 0.0 copy-start.3
  7.2 0.0 copy-start
  7.2 0.0 all-gather.11.cloned.1.call-start
  7.2 1.4 fusion.37
  14.5 2.6 constant_dynamic-slice_fusion.3
  17.2 0.0 all-gather.11.cloned.1.call-update
  17.2 0.0 all-gather.9.cloned.1.call-start
  17.2 0.7 all-gather.9.cloned.1.call-update
  17.9 0.0 all-gather.7.cloned.1.call-start
  18.0 0.7 all-gather.7.cloned.1.call-update
  18.7 0.0 copy-done.3
  18.7 0.0 copy-done
  18.7 0.5 copy.51
  19.3 3.7 gather_fusion.1
  23.0 3.7 broadcast_select_fusion.2
  26.7 0.9 copy.27
  27.6 7.3 %all-to-all-start = ((bf16[2,8,128,128]{3,2,0,1:T(8,128)(2,1)}), bf16[2,8,128,128]{3,2,0,1:T(8,128)(2,1)S(1)}, u32[]{:S(2)}, u32[]{:S(2)}) async-start(bf16[2,8,128,128]{3,2,0,1:T(8,128)(2,1)} %copy.27), calls=%async_computation | async-start | bytes 1048576 | tf_op jit(solution)/shard_map/all_to_all | solution.py:26
  34.9 25.4 %all-to-all-done = bf16[2,8,128,128]{3,2,0,1:T(8,128)(2,1)S(1)} async-done(((bf16[2,8,128,128]{3,2,0,1:T(8,128)(2,1)}), bf16[2,8,128,128]{3,2,0,1:T(8,128)(2,1)S(1)}, u32[]{:S(2)}, u32[]{:S(2)}) %all-to-all-start) | async-done | bytes 524320 | tf_op jit(solution)/shard_map/all_to_all | solution.py:26
  60.4 44.8 %all-gather.11.cloned.1.call-done = bf16[1,2,1024,1024]{3,2,1,0:T(8,128)(2,1)} async-done(((bf16[1,2,1024,128]{3,2,1,0:T(8,128)(2,1)}), bf16[1,2,1024,1024]{3,2,1,0:T(8,128)(2,1)}) %all-gather.11.cloned.1.call-update) | async-done | bytes 4194320 | tf_op jit(solution)/shard_map/all_gather | solution.py:34
  105.2 0.0 copy-start.6
  105.2 2.5 fusion.5
  107.7 2.4 fusion.28
  110.0 0.0 copy-done.6
  110.0 0.7 fusion.4
  110.8 0.8 fusion.29
  111.5 0.1 pad_maximum_fusion
  111.6 0.5 copy.30
  112.1 3.7 gather_fusion.2
  115.8 3.7 broadcast_select_fusion.1
  119.6 0.9 copy.31
  120.5 3.5 all-to-all-start.1
  124.0 23.9 %all-to-all-done.1 = bf16[2,8,128,128]{3,2,0,1:T(8,128)(2,1)S(1)} async-done(((bf16[2,8,128,128]{3,2,0,1:T(8,128)(2,1)}), bf16[2,8,128,128]{3,2,0,1:T(8,128)(2,1)S(1)}, u32[]{:S(2)}, u32[]{:S(2)}) %all-to-all-start.1) | async-done | bytes 524320 | tf_op jit(solution)/shard_map/all_to_all | solution.py:26
  148.0 43.0 %all-gather.9.cloned.1.call-done = bf16[1,2,1024,1024]{3,2,1,0:T(8,128)(2,1)} async-done(((bf16[1,2,1024,128]{3,2,1,0:T(8,128)(2,1)}), bf16[1,2,1024,1024]{3,2,1,0:T(8,128)(2,1)}) %all-gather.9.cloned.1.call-update) | async-done | bytes 4194320 | tf_op jit(solution)/shard_map/all_gather | solution.py:34
  191.0 0.0 copy-start.5
  191.0 2.5 fusion.3
  193.5 2.4 fusion.26
  195.9 0.0 copy-done.5
  195.9 0.7 fusion.2
  196.6 0.0 copy-start.1
  196.6 0.0 copy-start.2
  196.6 0.8 fusion.27
  197.4 0.1 pad_maximum_fusion.1
  197.4 0.5 copy.34
  198.0 3.7 gather_fusion.3
  201.7 3.7 broadcast_select_fusion
  205.4 0.9 copy.35
  206.3 3.7 all-to-all-start.2
  210.0 0.0 copy-done.1
  210.0 0.0 copy-done.2
  210.1 23.7 %all-to-all-done.2 = bf16[2,8,128,128]{3,2,0,1:T(8,128)(2,1)S(1)} async-done(((bf16[2,8,128,128]{3,2,0,1:T(8,128)(2,1)}), bf16[2,8,128,128]{3,2,0,1:T(8,128)(2,1)S(1)}, u32[]{:S(2)}, u32[]{:S(2)}) %all-to-all-start.2) | async-done | bytes 524320 | tf_op jit(solution)/shard_map/all_to_all | solution.py:26
  233.8 43.0 %all-gather.7.cloned.1.call-done = bf16[1,2,1024,1024]{3,2,1,0:T(8,128)(2,1)} async-done(((bf16[1,2,1024,128]{3,2,1,0:T(8,128)(2,1)}), bf16[1,2,1024,1024]{3,2,1,0:T(8,128)(2,1)}) %all-gather.7.cloned.1.call-update) | async-done | bytes 4194320 | tf_op jit(solution)/shard_map/all_gather | solution.py:34
  276.8 2.5 fusion.1
  279.3 2.3 fusion
  281.6 0.0 copy-done.4
  281.6 0.8 fusion.24
  282.4 0.7 fusion.25
  283.1 0.8 copy_bitcast_fusion
  284.0 0.8 pad_maximum_fusion.2
  284.8 1.2 pad_maximum_fusion.3
  286.0 20.2 %copy.38 = bf16[2,131072]{0,1:T(8,128)(2,1)} copy(bf16[2,131072]{1,0:T(2,128)(2,1)S(1)} %pad_maximum_fusion.3) | data formatting | bytes 1048576 | tf_op jit(solution)/shard_map/stack | solution.py:15
  306.2 21.6 %gather_fusion = bf16[2048,2]{1,0:T(8,128)(2,1)S(1)} fusion(bf16[2,131072]{0,1:T(8,128)(2,1)} %copy.38, s32[2048]{0:T(1024)S(1)} %broadcast_clamp_fusion), kind=kCustom, calls=%fused_computation.3 | custom fusion | bytes 24576 | tf_op jit(solution)/shard_map/jit(_take)/gather | solution.py:40
  327.9 0.7 select_bitcast_fusion
  328.6 49.9 %psum.7 = f32[2,2048]{0,1:T(8,128)S(1)} all-reduce(f32[2,2048]{0,1:T(8,128)S(1)} %select_bitcast_fusion), channel_id=1, replica_groups=mesh['cuts'=4,'mode'=8] {'cuts','mode'}, use_global_device_ids=true, to_apply=%region_0.0 | all-reduce | flops 4096 | bytes 32768 | tf_op jit(solution)/shard_map/psum | solution.py:42
  378.5 0.6 copy.39
  (14 shorter events, 0.2 us)
Async XLA Ops:
  7.2 11.5 %copy-start.3 = (s32[3,1024]{1,0:T(4,128)S(1)}, s32[3,1024]{1,0:T(4,128)}, u32[]{:S(2)}) copy-start(s32[3,1024]{1,0:T(4,128)} %param.11) | copy-start | bytes 36868
  7.2 11.5 %copy-start = (bf16[1,2,1024,128]{3,2,1,0:T(8,128)(2,1)S(1)}, bf16[1,2,1024,128]{3,2,1,0:T(8,128)(2,1)}, u32[]{:S(2)}) copy-start(bf16[1,2,1024,128]{3,2,1,0:T(8,128)(2,1)} %param.8) | copy-start | bytes 1572868
  7.2 98.0 %all-gather.11.cloned.1.call-start = ((), (), s32[]{:S(2)}) async-start(), calls=%async_computation.5 | async-start | bytes 4718592 | tf_op jit(solution)/shard_map/all_gather | solution.py:34
  17.2 173.8 %all-gather.9.cloned.1.call-start = ((), (), s32[]{:S(2)}) async-start(), calls=%async_computation.4 | async-start | bytes 4718592 | tf_op jit(solution)/shard_map/all_gather | solution.py:34
  17.9 258.9 %all-gather.7.cloned.1.call-start = ((), (), s32[]{:S(2)}) async-start(), calls=%async_computation.3 | async-start | bytes 4718592 | tf_op jit(solution)/shard_map/all_gather | solution.py:34
  27.6 32.7 %all-to-all-start = ((bf16[2,8,128,128]{3,2,0,1:T(8,128)(2,1)}), bf16[2,8,128,128]{3,2,0,1:T(8,128)(2,1)S(1)}, u32[]{:S(2)}, u32[]{:S(2)}) async-start(bf16[2,8,128,128]{3,2,0,1:T(8,128)(2,1)} %copy.27), calls=%async_computation | async-start | bytes 1048576 | tf_op jit(solution)/shard_map/all_to_all | solution.py:26
  105.2 4.9 %copy-start.6 = (bf16[1,2,1024,1024]{3,2,1,0:T(8,128)(2,1)S(1)}, bf16[1,2,1024,1024]{3,2,1,0:T(8,128)(2,1)}, u32[]{:S(2)}) copy-start(bf16[1,2,1024,1024]{3,2,1,0:T(8,128)(2,1)} %all-gather.11.cloned.1.call-done) | copy-start | bytes 12582916
  120.5 27.5 %all-to-all-start.1 = ((bf16[2,8,128,128]{3,2,0,1:T(8,128)(2,1)}), bf16[2,8,128,128]{3,2,0,1:T(8,128)(2,1)S(1)}, u32[]{:S(2)}, u32[]{:S(2)}) async-start(bf16[2,8,128,128]{3,2,0,1:T(8,128)(2,1)} %copy.31), calls=%async_computation.1 | async-start | bytes 1048576 | tf_op jit(solution)/shard_map/all_to_all | solution.py:26
  191.0 4.9 %copy-start.5 = (bf16[1,2,1024,1024]{3,2,1,0:T(8,128)(2,1)S(1)}, bf16[1,2,1024,1024]{3,2,1,0:T(8,128)(2,1)}, u32[]{:S(2)}) copy-start(bf16[1,2,1024,1024]{3,2,1,0:T(8,128)(2,1)} %all-gather.9.cloned.1.call-done) | copy-start | bytes 12582916
  196.6 13.4 %copy-start.1 = (s32[2048]{0:T(1024)S(1)}, s32[2048]{0:T(1024)}, u32[]{:S(2)}) copy-start(s32[2048]{0:T(1024)} %param.13) | copy-start | bytes 24580
  196.6 13.4 %copy-start.2 = (s32[2048]{0:T(1024)S(1)}, s32[2048]{0:T(1024)}, u32[]{:S(2)}) copy-start(s32[2048]{0:T(1024)} %param.12) | copy-start | bytes 24580
  206.3 27.4 %all-to-all-start.2 = ((bf16[2,8,128,128]{3,2,0,1:T(8,128)(2,1)}), bf16[2,8,128,128]{3,2,0,1:T(8,128)(2,1)S(1)}, u32[]{:S(2)}, u32[]{:S(2)}) async-start(bf16[2,8,128,128]{3,2,0,1:T(8,128)(2,1)} %copy.35), calls=%async_computation.2 | async-start | bytes 1048576 | tf_op jit(solution)/shard_map/all_to_all | solution.py:26
  276.8 4.8 %copy-start.4 = (bf16[1,2,1024,1024]{3,2,1,0:T(8,128)(2,1)S(1)}, bf16[1,2,1024,1024]{3,2,1,0:T(8,128)(2,1)}, u32[]{:S(2)}) copy-start(bf16[1,2,1024,1024]{3,2,1,0:T(8,128)(2,1)} %all-gather.7.cloned.1.call-done) | copy-start | bytes 12582916
Sparse Core Ops, SparseCore 0:
  17.3 87.8 all-gather.10
  107.2 83.7 all-gather.8
  193.0 83.7 all-gather.6
where the time goes:
time: 386 us
  waiting for transfers between devices  205 us (53%)
  local copies, waits for them, and re-layouts  62.9 us (16%)
  blocking collectives  49.9 us (13%)
  between operations  20 us (5%)
  matrix products  19 us (5%)
  starting transfers between devices  14.5 us (4%)
  other arithmetic  14.1 us (4%)
    all_gather x3, waiting for transfers between devices, body(): lax.all_gather(shard, 'mode', axis=2, tiled=True)  131 us
    all_to_all x3, waiting for transfers between devices, body(): lax.all_to_all(view, 'mode', split_axis=1, concat_axis=1, tiled=True)  73.1 us
    psum x1, blocking collectives, body(): total_amps = lax.psum(values, ('cuts', 'mode'))  49.9 us
    another operation x4, local copies, waits for them, and re-layouts, absorb(): return jnp.stack([real, imag], axis=0)  22.1 us
    gather x1, local copies, waits for them, and re-layouts, body(): values = jnp.take(flat, flat_index, axis=1).astype(jnp.float32)  21.6 us
    dot_general x12, matrix products, product(): lax.dot_general(left, right, numbers, preferred_element_type=jnp.float32)  19 us
    all_to_all x3, starting transfers between devices, body(): lax.all_to_all(view, 'mode', split_axis=1, concat_axis=1, tiled=True)  14.4 us
    select_n x3, other arithmetic, body(): moved = jnp.take(local, swap_order[step], axis=1)  11.2 us
  transfers between devices with their start and end apart: 6, of which 6 were waited for; matrix products, arithmetic and copies ran while one was open for 10% of the time, Pallas kernels for 0%

commit v1 on v0

v1 whole, which is shorter than its diff:
```python
import functools

import jax
import jax.numpy as jnp
from jax import lax
from jax.experimental import pallas as pl
from jax.experimental.pallas import tpu as pltpu
from jax.sharding import PartitionSpec as P

EVERY = ("cuts", "mode")
ROOM = 48 * 2**20


def vmem(count):
    return [pl.BlockSpec(memory_space=pltpu.VMEM)] * count


def one_hot(places, first, length):
    states = first + lax.broadcasted_iota(jnp.int32, (length, places.shape[1]), 0)
    return jnp.where(states == places, 1.0, 0.0).astype(jnp.bfloat16)


def dot(left, right, over_left=1):
    return lax.dot_general(left, right, (((over_left,), (0,)), ((), ())), preferred_element_type=jnp.float32)


def chunks_of(width):
    size = 256 if width % 256 == 0 else width
    return [slice(start, start + size) for start in range(0, width, size)]


def spread_kernel(stem, places, out):
    groups, _, block, width = out.shape
    for cut in chunks_of(width):
        choose = one_hot(places[:, cut], 0, width)
        for part in range(2):
            moved = dot(stem[part], choose, 0).astype(jnp.bfloat16)
            for m in range(groups):
                out[m, part, :, cut] = moved[m * block : (m + 1) * block]


def spread(stem, places, groups):
    _, width, rows = stem.shape
    return pl.pallas_call(
        spread_kernel,
        out_shape=jax.ShapeDtypeStruct((groups, 2, rows // groups, width), stem.dtype),
        in_specs=vmem(2),
        out_specs=vmem(1)[0],
        compiler_params=pltpu.CompilerParams(vmem_limit_bytes=ROOM),
    )(stem, places)


def step_kernel(plan, last, *refs):
    pick, field, places = refs[:3]
    pieces, (out, matrix, packed, semaphore) = refs[3:-4], refs[-4:]
    groups, _, block, width = field.shape
    low = width // groups
    rows = groups * block
    copies = [
        pltpu.make_async_copy(source(pieces, pick), matrix.at[where], semaphore.at[number])
        for number, (source, where) in enumerate(plan)
    ]
    for copy in copies:
        copy.start()
    for a in range(groups):
        for b in range(groups):
            real = field[a, 0, :, b * low : (b + 1) * low]
            imag = field[a, 1, :, b * low : (b + 1) * low]
            at, to = slice(b * block, (b + 1) * block), slice(a * low, (a + 1) * low)
            after = slice(width + a * low, width + (a + 1) * low)
            packed[at, to] = real
            packed[at, after] = -imag
            packed[rows + b * block : rows + (b + 1) * block, to] = imag
            packed[rows + b * block : rows + (b + 1) * block, after] = real
    for copy in copies:
        copy.wait()
    whole = []
    for cut in chunks_of(width):
        side = matrix[:, :, cut].reshape(2 * width, cut.stop - cut.start)
        whole.append(dot(packed[...], side).astype(jnp.bfloat16))
    result = jnp.concatenate(whole, axis=1)
    if last:
        for part in range(2):
            for c in range(groups):
                start = part * rows + c * block
                out[c, part] = result[start : start + block]
        return
    for cut in chunks_of(width):
        moved = dot(result, one_hot(places[:, cut], 0, width)).astype(jnp.bfloat16)
        for part in range(2):
            for c in range(groups):
                start = part * rows + c * block
                out[c, part, :, cut] = moved[start : start + block]


def step_of(plan, last, pick, field, places, pieces):
    groups, _, block, width = field.shape
    return pl.pallas_call(
        functools.partial(step_kernel, plan, last),
        out_shape=jax.ShapeDtypeStruct(field.shape, field.dtype),
        in_specs=[pl.BlockSpec(memory_space=pltpu.SMEM), *vmem(2)] + [pl.BlockSpec(memory_space=pl.ANY)] * len(pieces),
        out_specs=vmem(1)[0],
        scratch_shapes=[
            pltpu.VMEM((2, width, width), field.dtype),
            pltpu.VMEM((2 * groups * block, 2 * width), field.dtype),
            pltpu.SemaphoreType.DMA((len(plan),)),
        ],
        compiler_params=pltpu.CompilerParams(vmem_limit_bytes=ROOM),
    )(pick, field, places, *pieces)


def pick_kernel(field, states, spots, out):
    groups, _, block, width = field.shape
    rows = groups * block
    whole = jnp.concatenate([field[:, part].reshape(rows, width) for part in range(2)], axis=0)
    for cut in chunks_of(states.shape[1]):
        found = dot(whole, one_hot(states[:, cut], 0, width))
        here = lax.broadcasted_iota(jnp.int32, (rows, cut.stop - cut.start), 0) == spots[:, cut]
        for part in range(2):
            value = jnp.where(here, found[part * rows : (part + 1) * rows], 0.0)
            out[part : part + 1, cut] = jnp.sum(value, axis=0, keepdims=True)


def pick_entries(field, states, spots):
    return pl.pallas_call(
        pick_kernel,
        out_shape=jax.ShapeDtypeStruct((2, states.shape[1]), jnp.float32),
        in_specs=vmem(3),
        out_specs=vmem(1)[0],
        compiler_params=pltpu.CompilerParams(vmem_limit_bytes=ROOM),
    )(field, states, spots)


def collect_kernel(field, out):
    groups, _, block, width = field.shape
    for part in range(2):
        rows = field[:, part].reshape(groups * block, width)
        out[part] = jnp.transpose(rows)


def collect(field):
    groups, _, block, width = field.shape
    return pl.pallas_call(
        collect_kernel,
        out_shape=jax.ShapeDtypeStruct((2, width, groups * block), field.dtype),
        in_specs=vmem(1),
        out_specs=vmem(1)[0],
        compiler_params=pltpu.CompilerParams(vmem_limit_bytes=ROOM),
    )(field)


def add_up(values):
    devices = lax.axis_size(EVERY)
    share = values.shape[1] // devices
    blocks = values.reshape(2, devices, share).transpose(1, 0, 2)
    return jnp.sum(lax.all_to_all(blocks, EVERY, 0, 0), axis=0)


def batched(stem, branches, order, swap_order, row_bits, column_bits):
    local = stem[0]
    groups = lax.axis_size("mode")
    cuts = lax.axis_size("cuts")
    _, width, rows = local.shape
    block = rows // groups
    steps = swap_order.shape[0]
    places = [swap_order[step][None] for step in range(steps)]
    part = width // cuts
    own = lax.dynamic_slice_in_dim(branches, lax.axis_index("cuts") * part, part, 2)
    gathered = lax.all_gather(own, EVERY, axis=0)
    field = lax.all_to_all(spread(local, places[0], groups), "mode", 0, 0)
    plan = []
    for c in range(cuts):
        for g in range(groups):
            where = (slice(None), pl.ds(c * part, part), pl.ds(g * rows, rows))
            plan.append((lambda pieces, pick, at=c * groups + g: pieces[0].at[at, pick[0]], where))
    for step in range(steps):
        last = step == steps - 1
        field = step_of(plan, last, order[step][None], field, places[0 if last else step + 1], [gathered])
    low = column_bits % rows - lax.axis_index("mode") * block
    inside = jnp.logical_and(low >= 0, low < block)
    spots = jnp.where(inside, column_bits // rows * block + low, -1)
    values = pick_entries(field, row_bits[None], spots[None])
    result = collect(lax.all_to_all(field, "mode", 0, 0))
    return result[None], add_up(values)


def stepwise(stem, branches, order, swap_order, row_bits, column_bits):
    local = stem[0]
    groups = lax.axis_size("mode")
    _, width, rows = local.shape
    states = jnp.arange(width)[:, None]

    def product(left, right):
        return lax.dot_general(left, right, (((0,), (0,)), ((), ())), preferred_element_type=jnp.float32)

    for step in range(swap_order.shape[0]):
        choose = (states == swap_order[step][None]).astype(local.dtype)
        moved = jnp.stack([product(choose, local[part]).astype(local.dtype) for part in range(2)])
        view = moved.reshape(2, groups, width // groups, rows)
        swapped = lax.all_to_all(view, "mode", split_axis=1, concat_axis=1, tiled=True)
        field = swapped.reshape(2, width, rows)
        shard = lax.dynamic_index_in_dim(branches, order[step], 0, keepdims=False)
        matrix = lax.all_gather(shard, "mode", axis=2, tiled=True)
        real = product(matrix[0], field[0]) - product(matrix[1], field[1])
        imag = product(matrix[0], field[1]) + product(matrix[1], field[0])
        local = jnp.stack([real, imag]).astype(local.dtype)
    chosen = (states == row_bits[None]).astype(local.dtype)
    column = column_bits - lax.axis_index("mode") * rows
    here = jnp.arange(rows)[:, None] == column[None]
    values = jnp.stack([jnp.sum(jnp.where(here, product(local[part], chosen), 0.0), axis=0) for part in range(2)])
    return local[None], add_up(values)


def solution(mesh):
    groups, cuts = mesh.shape["mode"], mesh.shape["cuts"]

    def body(stem, branches, *rest):
        _, _, width, rows = stem.shape
        fits = rows % (16 * groups) == 0 and width % (128 * groups) == 0 and branches.shape[3] == rows
        fits = fits and rows % 128 == 0 and width % (16 * cuts) == 0
        return (batched if fits else stepwise)(stem, branches, *rest)

    return jax.shard_map(
        body,
        mesh=mesh,
        in_specs=(P("cuts", None, None, "mode"), P(None, None, None, "mode"), P(), P(), P(), P()),
        out_specs=(P("cuts", None, None, "mode"), P(None, EVERY)),
        check_vma=False,
    )
```

time: 386 us -> 169 us (0.44)
  waiting for transfers between devices: 205 us -> 108 us
  local copies, waits for them, and re-layouts: 62.9 us -> 4.42 us
  blocking collectives: 49.9 us -> 9.76 us
  Pallas kernels: 0 us -> 20.3 us
  matrix products: 19 us -> 0 us
  other arithmetic: 14.1 us -> 1.3 us
  between operations: 20 us -> 14.1 us
    all_gather x3 -> x1, waiting for transfers between devices: 131 us -> 73.5 us  [batched(): gathered = lax.all_gather(own, EVERY, axis=0)]
    psum x1 -> x0, blocking collectives: 49.9 us -> none  [body(): total_amps = lax.psum(values, ('cuts', 'mode'))]
    all_to_all x3 -> x2, waiting for transfers between devices: 73.1 us -> 34.7 us  [the longest x1 21.9 us: batched(): field = lax.all_to_all(spread(local, places[0], groups), 'mode', 0, 0)]
    gather x4 -> x0, local copies, waits for them, and re-layouts: 32.7 us -> none  [the longest x1 21.6 us: body(): values = jnp.take(flat, flat_index, axis=1).astype(jnp.float32)]
    another operation x4 -> x0, local copies, waits for them, and re-layouts: 22.1 us -> none  [absorb(): return jnp.stack([real, imag], axis=0)]
    pallas_call x0 -> x6, Pallas kernels: none -> 20.3 us  [the longest x3 15.1 us: step_of(): pl.pallas_call(functools.partial(step_kernel, plan, last), out_shape=jax....]
    dot_general x12 -> x0, matrix products: 19 us -> none  [product(): lax.dot_general(left, right, numbers, preferred_element_type=jnp.float32)]
    select_n x4 -> x1, other arithmetic: 11.9 us -> 0.01 us  [batched(): spots = jnp.where(inside, column_bits // rows * block + low, -1)]
  transfers between devices with their start and end apart: 6 -> 3, of which waited for: 6 -> 3; matrix products, arithmetic and copies ran while one was open for 10% -> 2% of each run, Pallas kernels for 0% -> 1%
where the time goes in v1:
time: 169 us
  waiting for transfers between devices  108 us (64%)
  Pallas kernels  20.3 us (12%)
  between operations  14.1 us (8%)
  starting transfers between devices  10.8 us (6%)
  blocking collectives  9.76 us (6%)
  local copies, waits for them, and re-layouts  4.42 us (3%)
    all_gather x1, waiting for transfers between devices, batched(): gathered = lax.all_gather(own, EVERY, axis=0)  73.5 us
    all_to_all x1, waiting for transfers between devices, batched(): field = lax.all_to_all(spread(local, places[0], groups), 'mode', 0, 0)  21.9 us
    pallas_call x3, Pallas kernels, step_of(): pl.pallas_call(functools.partial(step_kernel, plan, last), out_shape=jax....  15.1 us
    all_to_all x1, waiting for transfers between devices, batched(): result = collect(lax.all_to_all(field, 'mode', 0, 0))  12.8 us
    all_to_all x1, blocking collectives, add_up(): return jnp.sum(lax.all_to_all(blocks, EVERY, 0, 0), axis=0)  9.76 us
    all_to_all x1, starting transfers between devices, batched(): field = lax.all_to_all(spread(local, places[0], groups), 'mode', 0, 0)  7.25 us
    all_to_all x1, starting transfers between devices, batched(): result = collect(lax.all_to_all(field, 'mode', 0, 0))  3.49 us
  transfers between devices with their start and end apart: 3, of which 3 were waited for; matrix products, arithmetic and copies ran while one was open for 2% of the time, Pallas kernels for 1%

profile of v1, /device:TPU:0, one launch (start us, length us, event | category | flops | bytes accessed | tf_op | source)
XLA Modules:
  0.0 169.0 jit_solution(13774971446734380372)
XLA Ops:
  7.2 0.0 copy-start
  7.2 0.0 copy-start.1
  7.2 0.0 all-gather.3.cloned.1.call-start
  7.2 1.3 copy-done
  8.6 0.0 copy-start.4
  8.6 0.0 copy-start.3
  8.6 0.8 constant_dynamic-slice_fusion
  9.4 0.0 all-gather.3.cloned.1.call-update
  9.4 0.8 fusion.6
  10.3 0.0 copy-done.1
  10.3 1.6 shard_map.77
  11.8 7.2 %all-to-all-start = ((bf16[8,2,16,1024]{3,2,1,0:T(8,128)(2,1)}), bf16[8,2,16,1024]{3,2,1,0:T(8,128)(2,1)S(1)}, u32[]{:S(2)}, u32[]{:S(2)}) async-start(bf16[8,2,16,1024]{3,2,1,0:T(8,128)(2,1)} %shard_map.77), calls=%async_computation | async-start | bytes 1048576 | tf_op jit(solution)/shard_map/all_to_all | solution.py:170
  19.1 0.0 copy-done.4
  19.1 0.6 fusion.7
  19.7 0.0 copy-done.3
  19.7 21.9 %all-to-all-done.refs_1_ = bf16[8,2,16,1024]{3,2,1,0:T(8,128)(2,1)S(1)} async-done(((bf16[8,2,16,1024]{3,2,1,0:T(8,128)(2,1)}), bf16[8,2,16,1024]{3,2,1,0:T(8,128)(2,1)S(1)}, u32[]{:S(2)}, u32[]{:S(2)}) %all-to-all-start) | async-done | bytes 524320 | tf_op jit(solution)/shard_map/all_to_all | solution.py:170
  41.6 73.5 %all-gather.3.cloned.1.call-done = bf16[96,2,256,128]{3,2,1,0:T(8,128)(2,1)} async-done(((bf16[3,2,256,128]{3,2,1,0:T(8,128)(2,1)}), bf16[96,2,256,128]{3,2,1,0:T(8,128)(2,1)}) %all-gather.3.cloned.1.call-update) | async-done | bytes 12582928 | tf_op jit(solution)/shard_map/all_gather | solution.py:169
  115.2 5.0 %shard_map.78.refs_1_ = bf16[8,2,16,1024]{3,2,1,0:T(8,128)(2,1)S(1)} custom-call(s32[1]{0:T(128)} %get-tuple-element.5.refs_0_, bf16[8,2,16,1024]{3,2,1,0:T(8,128)(2,1)S(1)} %all-to-all-done.refs_1_, s32[1,1024]{1,0:T(1,128)S(1)} %get-tuple-element.4.refs_2_, bf16[32,3,2,256,128]{4,3,2,1,0:T(8,128)(2,1)} %bitcast.11), custom_call_target="tpu_custom_call" | custom-call | tf_op jit(solution)/shard_map/pallas_call | solution.py:98
  120.2 5.0 %shard_map.79.refs_1_ = bf16[8,2,16,1024]{3,2,1,0:T(8,128)(2,1)S(1)} custom-call(s32[1]{0:T(128)} %get-tuple-element.7.refs_0_, bf16[8,2,16,1024]{3,2,1,0:T(8,128)(2,1)S(1)} %shard_map.78.refs_1_, s32[1,1024]{1,0:T(1,128)S(1)} %get-tuple-element.2.refs_2_, bf16[32,3,2,256,128]{4,3,2,1,0:T(8,128)(2,1)} %bitcast.12), custom_call_target="tpu_custom_call" | custom-call | tf_op jit(solution)/shard_map/pallas_call | solution.py:98
  125.1 0.0 copy-start.2
  125.2 5.2 %shard_map.80.field = bf16[8,2,16,1024]{3,2,1,0:T(8,128)(2,1)} custom-call(s32[1]{0:T(128)} %get-tuple-element.6.refs_0_, bf16[8,2,16,1024]{3,2,1,0:T(8,128)(2,1)S(1)} %shard_map.79.refs_1_, s32[1,1024]{1,0:T(1,128)S(1)} %get-tuple-element.3.places.refs_2_, bf16[32,3,2,256,128]{4,3,2,1,0:T(8,128)(2,1)} %bitcast.13), custom_call_target="tpu_custom_call" | custom-call | tf_op jit(solution)/shard_map/pallas_call | solution.py:98
  130.3 0.0 copy-done.2
  130.3 2.6 %shard_map.82 = f32[2,2048]{1,0:T(2,128)S(1)} custom-call(bf16[8,2,16,1024]{3,2,1,0:T(8,128)(2,1)} %shard_map.80.field, s32[1,2048]{1,0:T(1,128)S(1)} %bitcast.10, s32[1,2048]{1,0:T(1,128)S(1)} %bitcast.9), custom_call_target="tpu_custom_call" | custom-call | tf_op jit(solution)/shard_map/pallas_call | solution.py:125
  132.9 0.1 reshape.7
  133.1 0.1 reshape.9
  133.2 9.8 %all_to_all.15 = f32[32,1,128]{2,1,0:T(1,128)S(1)} all-to-all(f32[32,1,128]{2,1,0:T(1,128)S(1)} %reshape.9), channel_id=1, replica_groups=mesh['cuts'=4,'mode'=8] {'cuts','mode'}, dimensions={0} | all-to-all | bytes 32768 | tf_op jit(solution)/shard_map/all_to_all | solution.py:156
  142.9 3.5 %all-to-all-start.1 = ((bf16[8,2,16,1024]{3,2,1,0:T(8,128)(2,1)}), bf16[8,2,16,1024]{3,2,1,0:T(8,128)(2,1)S(1)}, u32[]{:S(2)}, u32[]{:S(2)}) async-start(bf16[8,2,16,1024]{3,2,1,0:T(8,128)(2,1)} %shard_map.80.field), calls=%async_computation.1 | async-start | bytes 1048576 | tf_op jit(solution)/shard_map/all_to_all | solution.py:183
  146.4 0.5 broadcast.18
  147.0 0.7 reduce
  147.6 0.1 reshape.10
  147.7 0.6 reduce_sum.9
  148.3 12.8 %all-to-all-done.1.field = bf16[8,2,16,1024]{3,2,1,0:T(8,128)(2,1)S(1)} async-done(((bf16[8,2,16,1024]{3,2,1,0:T(8,128)(2,1)}), bf16[8,2,16,1024]{3,2,1,0:T(8,128)(2,1)S(1)}, u32[]{:S(2)}, u32[]{:S(2)}) %all-to-all-start.1) | async-done | bytes 524320 | tf_op jit(solution)/shard_map/all_to_all | solution.py:183
  161.1 1.0 shard_map.81
  (2 shorter events, 0.0 us)
Async XLA Ops:
  7.2 1.4 copy-start
  7.2 3.1 %copy-start.1 = (bf16[1,2,1024,128]{3,2,1,0:T(8,128)(2,1)S(1)}, bf16[1,2,1024,128]{3,2,1,0:T(8,128)(2,1)}, u32[]{:S(2)}) copy-start(bf16[1,2,1024,128]{3,2,1,0:T(8,128)(2,1)} %param.6) | copy-start | bytes 1572868
  7.2 108.0 %all-gather.3.cloned.1.call-start = ((), (), s32[]{:S(2)}) async-start(), calls=%async_computation.3 | async-start | bytes 12976128 | tf_op jit(solution)/shard_map/all_gather | solution.py:169
  8.6 10.5 %copy-start.4 = (s32[3]{0:T(128)S(1)}, s32[3]{0:T(128)}, u32[]{:S(2)}) copy-start(s32[3]{0:T(128)} %param.8) | copy-start | bytes 40
  8.6 11.1 %copy-start.3 = (s32[2048]{0:T(1024)S(1)}, s32[2048]{0:T(1024)}, u32[]{:S(2)}) copy-start(s32[2048]{0:T(1024)} %param.11) | copy-start | bytes 24580
  11.8 29.8 %all-to-all-start = ((bf16[8,2,16,1024]{3,2,1,0:T(8,128)(2,1)}), bf16[8,2,16,1024]{3,2,1,0:T(8,128)(2,1)S(1)}, u32[]{:S(2)}, u32[]{:S(2)}) async-start(bf16[8,2,16,1024]{3,2,1,0:T(8,128)(2,1)} %shard_map.77), calls=%async_computation | async-start | bytes 1048576 | tf_op jit(solution)/shard_map/all_to_all | solution.py:170
  125.1 5.2 %copy-start.2 = (s32[2048]{0:T(1024)S(1)}, s32[2048]{0:T(1024)}, u32[]{:S(2)}) copy-start(s32[2048]{0:T(1024)} %param.10) | copy-start | bytes 24580
  142.9 18.2 %all-to-all-start.1 = ((bf16[8,2,16,1024]{3,2,1,0:T(8,128)(2,1)}), bf16[8,2,16,1024]{3,2,1,0:T(8,128)(2,1)S(1)}, u32[]{:S(2)}, u32[]{:S(2)}) async-start(bf16[8,2,16,1024]{3,2,1,0:T(8,128)(2,1)} %shard_map.80.field), calls=%async_computation.1 | async-start | bytes 1048576 | tf_op jit(solution)/shard_map/all_to_all | solution.py:183
Sparse Core Ops, SparseCore 0:
  11.0 104.1 all-gather.2
